TPU v7x, 32 devices: a whole 2x2x4 slice. The times are simulated.
32 devices in a mesh: groups: 2 (over y), rows: 4 (over z), edges: 2 (over x), cols: 2 (over core).
Axes of the slice: x: 2, y: 2, z: 4, core: 2. Of those that a mesh axis runs over, the one named last changes fastest.
Arguments:
- entities: float32 [16384, 400], P(('groups', 'rows'), 'cols'), parts along dimension 0, may hold values from -1.8 to 1.8
- entity_state: float32 [16384], P(('groups', 'rows')), parts along dimension 0, may hold values from 0.001 to 0.01
- relations: float32 [6144, 400], P('groups', 'cols'), parts along dimension 0, may hold values from -6 to 6
- relation_state: float32 [6144], P('groups'), parts along dimension 0, may hold values from 0.001 to 0.01
- requests: int32 [8, 4, 2, 2, 64], P(('groups', 'rows'), None, 'edges'), parts along dimension 0, may hold values from -1 to 2047, as said below
- head_slot: int32 [8, 2, 2, 1024], P(('groups', 'rows'), 'edges', None, 'cols'), parts along dimension 0, may hold values from 0 to 255, as said below
- tail_slot: int32 [8, 2, 2, 1024], P(('groups', 'rows'), 'edges', None, 'cols'), parts along dimension 0, may hold values from 0 to 255, as said below
- relation_ids: int32 [8, 2, 2, 1024], P(('groups', 'rows'), 'edges', None, 'cols'), parts along dimension 0, may hold values from 0 to 3071
- negative_slot: int32 [8, 2, 2, 1536], P(('groups', 'rows'), 'edges'), parts along dimension 0, may hold values from 0 to 255, as said below
Outputs:
- new_entities: float32 [16384, 400], P(('groups', 'rows'), 'cols'), parts along dimension 0
- new_entity_state: float32 [16384], P(('groups', 'rows')), parts along dimension 0
- new_relations: float32 [6144, 400], P('groups', 'cols'), parts along dimension 0
- new_relation_state: float32 [6144], P('groups'), parts along dimension 0
There are 2 independent parts, one for each index of `groups`. A program takes and returns all parts, laid end to end along the dimension named above; each array names one. Nothing has to cross between parts.
Inputs may be any that keep to these rules, and one draw needn't show every extreme that they name: requests[o, r, e, k, j] is a row of shard o or -1 for an empty slot; the ids of one list are distinct and the live ones come first; every list holds 16 or more live ids, and for each worker and block the list of one owner is full. `head_slot`: each value is o * 64 + j with j below the number of live ids in owner o's list for that worker and block. `tail_slot`: each value is o * 64 + j with j below the number of live ids in owner o's list for that worker and block. `negative_slot`: each value is o * 64 + j with j below the number of live ids in owner o's list for that worker and block.
All inputs are finite; a program needn't handle non-finite values.
Results may differ from a plain program's by a relative error of at most 0.0031.
Values may be sent and summed in bfloat16 or wider, within the bound.
A program may use at most 128 MiB of HBM per device.

v0:
```python
import functools

import jax
import jax.numpy as jnp
from jax import lax
from jax.experimental import pallas as pl
from jax.experimental.pallas import tpu as pltpu
from jax.sharding import PartitionSpec as P

LEARNING = 0.3
F32 = jnp.float32
BF16 = jnp.bfloat16
NT = (((1,), (1,)), ((), ()))
TN = (((0,), (0,)), ((), ()))


def dot(a, b):
    return jnp.dot(a, b, preferred_element_type=F32)


def dot_nt(a, b):
    return lax.dot_general(a, b, NT, preferred_element_type=F32)


def dot_tn(a, b):
    return lax.dot_general(a, b, TN, preferred_element_type=F32)


def one_hot(start, count, ids):
    rows = lax.broadcasted_iota(jnp.int32, (count, ids.shape[1]), 0) + start
    return jnp.where(rows == ids, 1.0, 0.0).astype(BF16)


def neighbours(x):
    grouped = x.reshape(x.shape[0] // 8, 8, x.shape[1])
    after = pltpu.roll(grouped, 7, 1).reshape(x.shape)
    before = pltpu.roll(grouped, 1, 1).reshape(x.shape)
    return after, before


def split_high(x):
    high = x.astype(BF16)
    return high, (x - high.astype(F32)).astype(BF16)


def pad_rows(x, rows):
    return jnp.concatenate([x, jnp.zeros((rows - x.shape[0], x.shape[1]), x.dtype)], axis=0)


def when(static, condition):
    if static:
        return lambda body: body()
    return pl.when(condition)


def kernel(
    n, ent, est, rel, rst, req, head, tail, rid, neg,
    new_ent, new_est, new_rel, new_rst,
    relb, entb, fetg, fet, allreq, oh_head, oh_tail, oh_rel, share, rho, rho_hi, rho_lo,
    slot_grad, ent_send, ent_in, grad_out, grad_in, sq_ent, sq_ent_in,
    pair_out, pair_in, pair_sum, x_out, x_in, z_out, z_in, total, sq_rel, sq_rel_in,
    s_relb, r_relb, s_req, r_req, s_fet, r_fet, s_ent, r_ent, s_grad, r_grad,
    s_pair, r_pair, s_x, r_x, s_z, r_z, s_agz, r_agz, s_agx, r_agx, s_sq, r_sq,
):
    R, E, K, PW, L, PIECES, HP = n.rows, n.edges, n.blocks, n.width, n.lanes, n.pieces, n.padded
    r, e, c = lax.axis_index("rows"), lax.axis_index("edges"), lax.axis_index("cols")
    pc = 1 - c
    half = ent.shape[0]
    full = PIECES == R

    def remote(src, dst, s_sem, r_sem, row, edge, col):
        return pltpu.make_async_remote_copy(
            src_ref=src, dst_ref=dst, send_sem=s_sem, recv_sem=r_sem,
            device_id={"rows": row, "edges": edge, "cols": col},
            device_id_type=pl.DeviceIdType.MESH,
        )

    barrier = pltpu.get_barrier_semaphore()
    for dr in range(R):
        for de in range(E):
            for dc in range(2):
                if dr or de or dc:
                    pl.semaphore_signal(
                        barrier, inc=1,
                        device_id={
                            "rows": lax.rem(r + dr, R),
                            "edges": lax.rem(e + de, E),
                            "cols": lax.rem(c + dc, 2),
                        },
                        device_id_type=pl.DeviceIdType.MESH,
                    )
    sent = []

    entb[...] = pad_rows(ent[...], HP).astype(BF16)
    relb[c] = pad_rows(rel[...], HP).astype(BF16)
    allreq[e] = req[...]
    for w in range(R):
        ids = req[:, w * PW : (w + 1) * PW]
        fetg[w] = dot(entb[...], one_hot(0, ent.shape[1], ids)).astype(BF16)
    pl.semaphore_wait(barrier, R * E * 2 - 1)

    fetch = []
    for dr in range(R):
        row = lax.rem(r + dr, R)
        here = fet.at[c, :, pl.ds(pl.multiple_of(r * PW, PW), PW)]
        for dc in range(2):
            if dr or dc:
                i = dr * 2 + dc - 1
                copy = remote(fetg.at[row], here, s_fet.at[i], r_fet.at[i], row, e, lax.rem(c + dc, 2))
                copy.start()
                fetch.append(copy)
    fet[c, :, pl.ds(pl.multiple_of(r * PW, PW), PW)] = fetg[r]
    relation_copy = remote(relb.at[c], relb.at[c], s_relb.at[0], r_relb.at[0], r, e, pc)
    relation_copy.start()
    request_copies = []
    for de in range(1, E):
        copy = remote(
            allreq.at[e], allreq.at[e], s_req.at[de - 1], r_req.at[de - 1], r, lax.rem(e + de, E), c
        )
        copy.start()
        request_copies.append(copy)
    sent += fetch + [relation_copy] + request_copies

    positions = R * PW
    negatives = neg.shape[1] // K
    for k in range(K):
        slots = lax.broadcasted_iota(jnp.int32, (positions, 128), 0)
        hits = jnp.zeros((positions, 128), F32)
        for at in range(k * negatives, (k + 1) * negatives, 128):
            hits += jnp.where(slots == neg[:, at : at + 128], 1.0, 0.0)
        share[k] = jnp.sum(hits, axis=1, keepdims=True) / negatives

    edges = head.shape[1]
    step = n.step

    @pl.loop(0, edges // step)
    def _(t):
        cols = pl.ds(pl.multiple_of(t * step, step), step)
        oh_head[:, cols] = one_hot(0, positions, head[:, cols])
        oh_tail[:, cols] = one_hot(0, positions, tail[:, cols])
        oh_rel[:, cols] = one_hot(0, rel.shape[1], rid[:, cols])
        rho[c, :, cols] = dot(relb[c], oh_rel[:, cols]).astype(BF16)

    relation_copy.wait_recv()

    @pl.loop(0, edges // step)
    def _(t):
        cols = pl.ds(pl.multiple_of(t * step, step), step)
        rho[pc, :, cols] = dot(relb[pc], oh_rel[:, cols]).astype(BF16)

    for copy in fetch:
        copy.wait_recv()

    slot_grad[...] = jnp.zeros_like(slot_grad)
    per_block = edges // K
    for k in range(K):

        @pl.loop(0, per_block // step)
        def _(t):
            cols = pl.ds(pl.multiple_of(k * per_block + t * step, step), step)
            rows = fet[...].reshape(2 * HP, positions)
            h = dot(rows, oh_head[:, cols])
            tl = dot(rows, oh_tail[:, cols])
            rh = rho[:, :, cols].reshape(2 * HP, step).astype(F32)
            even = lax.rem(lax.broadcasted_iota(jnp.int32, (2 * HP, step), 0), 2) == 0
            h_after, h_before = neighbours(h)
            r_after, r_before = neighbours(rh)
            r_re = jnp.where(even, rh, r_before)
            r_im = jnp.where(even, -r_after, rh)
            query = h * r_re + jnp.where(even, h_after, h_before) * r_im
            query_b = query.astype(BF16)
            positive = jnp.sum(query * tl, axis=0, keepdims=True)
            pos_weight = -jax.nn.sigmoid(-positive)
            scores = dot_tn(rows, query_b)
            weight = (jax.nn.sigmoid(scores) * share[k]).astype(BF16)
            g = pos_weight * tl + dot(rows, weight)
            g_after, g_before = neighbours(g)
            g_swap = jnp.where(even, g_after, g_before)
            head_grad = g * r_re - g_swap * r_im
            h_re = jnp.where(even, h, h_before)
            h_im = jnp.where(even, -h_after, h)
            rho_grad = g * h_re - g_swap * h_im
            high, low = split_high(rho_grad)
            rho_hi[:, :, cols] = high.reshape(2, HP, step)
            rho_lo[:, :, cols] = low.reshape(2, HP, step)
            acc = dot_nt(query_b, weight)
            high, low = split_high(head_grad)
            acc += dot_nt(high, oh_head[:, cols]) + dot_nt(low, oh_head[:, cols])
            high, low = split_high(pos_weight * query)
            acc += dot_nt(high, oh_tail[:, cols]) + dot_nt(low, oh_tail[:, cols])
            slot_grad[...] += acc.reshape(2, HP, positions)

    ent_send[...] = slot_grad[pc]
    entity_pair = remote(ent_send, ent_in, s_ent.at[0], r_ent.at[0], r, e, pc)
    entity_pair.start()
    sent.append(entity_pair)

    def place(de, p):
        return pl.multiple_of((lax.rem(e + de, E) * PIECES + p) * L, L)

    order = [(de, p) for de in list(range(1, E)) + [0] for p in range(PIECES)]
    pairs = {}

    def dense(which, de, p):
        hot = oh_rel[pl.ds(place(de, p), L), :]
        return dot_nt(rho_hi[which], hot) + dot_nt(rho_lo[which], hot)

    def send_pair(de, p):
        i = de * PIECES + p
        pair_out[i] = dense(pc, de, p)
        copy = remote(pair_out.at[i], pair_in.at[i], s_pair.at[i], r_pair.at[i], r, e, pc)
        copy.start()
        pairs[de, p] = copy
        sent.append(copy)

    def x_copy(de, p):
        i = (de - 1) * PIECES + p
        return remote(x_out.at[i], x_in.at[i], s_x.at[i], r_x.at[i], r, lax.rem(e + de, E), c)

    def entity_out():
        entity_pair.wait_recv()
        summed = (slot_grad[c] + ent_in[...]).astype(BF16)
        for o in range(R):
            grad_out[o] = summed[:, o * PW : (o + 1) * PW]
        copies = []
        for dr in range(R):
            row = lax.rem(r + dr, R)
            for de in range(E):
                if dr or de:
                    i = dr * E + de - 1
                    copy = remote(
                        grad_out.at[row],
                        grad_in.at[e, :, pl.ds(pl.multiple_of(r * PW, PW), PW)],
                        s_grad.at[i], r_grad.at[i], row, lax.rem(e + de, E), c,
                    )
                    copy.start()
                    copies.append(copy)
        grad_in[e, :, pl.ds(pl.multiple_of(r * PW, PW), PW)] = grad_out[r]
        sent.extend(copies)
        return copies

    send_pair(*order[0])
    for at, (de, p) in enumerate(order):
        if at + 1 < len(order):
            send_pair(*order[at + 1])
        own = dense(c, de, p)
        pairs[de, p].wait_recv()
        own += pair_in[de * PIECES + p]
        if de:
            x_out[(de - 1) * PIECES + p] = own.astype(BF16)
            copy = x_copy(de, p)
            copy.start()
            sent.append(copy)
        else:
            pair_sum[p] = own
    grads = entity_out()

    def over_edges(p):
        acc = pair_sum[p]
        for de in range(1, E):
            x_copy(de, p).wait_recv()
            acc += x_in[(de - 1) * PIECES + p].astype(F32)
        return acc

    def z_copy(dr):
        return remote(
            z_out.at[dr - 1], z_in.at[dr - 1], s_z.at[dr - 1], r_z.at[dr - 1], lax.rem(r + dr, R), e, c
        )

    for dr in range(1, R):
        p = lax.rem(r + dr, R)

        @when(full, p < PIECES)
        def _():
            z_out[dr - 1] = over_edges(p).astype(BF16)
            z_copy(dr).start()

    def mine(dr):
        return e * PIECES + lax.rem(r + R - dr, R)

    def agz_copy(dr):
        return remote(
            total.at[mine(0)], total.at[mine(0)], s_agz.at[dr - 1], r_agz.at[dr - 1],
            lax.rem(r + dr, R), e, c,
        )

    def agx_copy(dr, de):
        i = dr * (E - 1) + de - 1
        return remote(
            total.at[mine(dr)], total.at[mine(dr)], s_agx.at[i], r_agx.at[i],
            r, lax.rem(e + de, E), c,
        )

    @when(full, r < PIECES)
    def _():
        acc = over_edges(r)
        for dr in range(1, R):
            z_copy(dr).wait_recv()
            acc += z_in[dr - 1].astype(F32)
        total[mine(0)] = acc.astype(BF16)
        for dr in range(1, R):
            agz_copy(dr).start()
        for de in range(1, E):
            agx_copy(0, de).start()

    for copy in request_copies + grads:
        copy.wait_recv()
    tile = n.tile

    @pl.loop(0, ent.shape[1] // tile)
    def _(t):
        cols = pl.ds(pl.multiple_of(t * tile, tile), tile)
        acc = jnp.zeros((HP, tile), F32)
        for edge in range(E):
            acc += dot_nt(grad_in[edge], one_hot(t * tile, tile, allreq[edge]))
        new_ent[:, cols] = acc[:half, :]
        sq_ent[:, cols] = jnp.sum(acc * acc, axis=0, keepdims=True)

    squares = remote(sq_ent, sq_ent_in, s_sq.at[0], r_sq.at[0], r, e, pc)
    squares.start()
    sent.append(squares)

    for dr in range(1, R):

        @when(full, lax.rem(r + R - dr, R) < PIECES)
        def _():
            agz_copy(dr).wait_recv()
            for de in range(1, E):
                agx_copy(dr, de).start()

    squares.wait_recv()
    state = est[...] + (sq_ent[...] + sq_ent_in[...]) / (2 * half)
    new_est[...] = state
    new_ent[...] = ent[...] - new_ent[...] * (LEARNING / jnp.sqrt(state))

    for dr in range(R):
        for de in range(1, E):

            @when(full, lax.rem(r + R - dr, R) < PIECES)
            def _():
                agx_copy(dr, de).wait_recv()

    for i in range(E * PIECES):
        g = total[i].astype(F32)
        sq_rel[:, i * L : (i + 1) * L] = jnp.sum(g * g, axis=0, keepdims=True)
    squares = remote(sq_rel, sq_rel_in, s_sq.at[1], r_sq.at[1], r, e, pc)
    squares.start()
    sent.append(squares)
    squares.wait_recv()
    state = rst[...] + (sq_rel[...] + sq_rel_in[...]) / (2 * half)
    new_rst[...] = state
    scale = LEARNING / jnp.sqrt(state)
    for i in range(E * PIECES):
        at = slice(i * L, (i + 1) * L)
        new_rel[:, at] = rel[:, at] - total[i].astype(F32)[:half, :] * scale[:, at]

    for copy in sent:
        copy.wait_send()
    for dr in range(1, R):

        @when(full, lax.rem(r + dr, R) < PIECES)
        def _():
            z_copy(dr).wait_send()

        @when(full, r < PIECES)
        def _():
            agz_copy(dr).wait_send()

    for dr in range(R):
        for de in range(1, E):

            @when(full, lax.rem(r + R - dr, R) < PIECES)
            def _():
                agx_copy(dr, de).wait_send()


class Sizes:
    pass


def local(
    entities, entity_state, relations, relation_state, requests,
    head_slot, tail_slot, relation_ids, negative_slot,
):
    n = Sizes()
    n.rows, n.edges = lax.axis_size("rows"), lax.axis_size("edges")
    n.blocks = requests.shape[3]
    capacity = requests.shape[4]
    shard_rows, half = entities.shape
    types = relations.shape[0]
    n.width = n.blocks * capacity
    n.padded = -(-half // 16) * 16
    n.lanes = -(-types // (n.rows * n.edges * 128)) * 128
    n.pieces = types // (n.edges * n.lanes)
    n.step = 256 if n.rows * n.width <= 1024 else 128
    n.tile = 256
    positions = n.rows * n.width
    edges = n.blocks * head_slot.shape[3]

    def spots(slots):
        slots = slots[0, 0]
        block = jnp.arange(n.blocks, dtype=jnp.int32)[:, None]
        return ((slots // capacity) * n.width + block * capacity + slots % capacity).reshape(1, -1)

    HP, R, E, PC, L = n.padded, n.rows, n.edges, n.pieces, n.lanes
    V = pltpu.VMEM
    sem = lambda k: pltpu.SemaphoreType.DMA((max(k, 1),))
    scratch = [
        V((2, HP, types), BF16), V((HP, shard_rows), BF16), V((R, HP, n.width), BF16),
        V((2, HP, positions), BF16), V((E, 1, positions), jnp.int32),
        V((positions, edges), BF16), V((positions, edges), BF16), V((types, edges), BF16),
        V((n.blocks, positions, 1), F32), V((2, HP, edges), BF16),
        V((2, HP, edges), BF16), V((2, HP, edges), BF16),
        V((2, HP, positions), F32), V((HP, positions), F32), V((HP, positions), F32),
        V((R, HP, n.width), BF16), V((E, HP, positions), BF16),
        V((1, shard_rows), F32), V((1, shard_rows), F32),
        V((E * PC, HP, L), F32), V((E * PC, HP, L), F32), V((PC, HP, L), F32),
        V((max((E - 1) * PC, 1), HP, L), BF16), V((max((E - 1) * PC, 1), HP, L), BF16),
        V((max(R - 1, 1), HP, L), BF16), V((max(R - 1, 1), HP, L), BF16),
        V((E * PC, HP, L), BF16), V((1, types), F32), V((1, types), F32),
    ]
    for count in (1, E - 1, 2 * R - 1, 1, R * E - 1, E * PC, (E - 1) * PC, R - 1, R - 1, R * (E - 1), 2):
        scratch += [sem(count), sem(count)]
    vm = pl.BlockSpec(memory_space=pltpu.VMEM)
    new_ent, new_est, new_rel, new_rst = pl.pallas_call(
        functools.partial(kernel, n),
        out_shape=[
            jax.ShapeDtypeStruct((half, shard_rows), F32),
            jax.ShapeDtypeStruct((1, shard_rows), F32),
            jax.ShapeDtypeStruct((half, types), F32),
            jax.ShapeDtypeStruct((1, types), F32),
        ],
        in_specs=[vm] * 9,
        out_specs=[vm] * 4,
        scratch_shapes=scratch,
        compiler_params=pltpu.CompilerParams(
            collective_id=0, has_side_effects=True, vmem_limit_bytes=60 * 2**20
        ),
        name="complex_step",
    )(
        entities.T, entity_state.reshape(1, -1), relations.T, relation_state.reshape(1, -1),
        requests.reshape(1, -1), spots(head_slot), spots(tail_slot),
        relation_ids.reshape(1, -1), spots(negative_slot),
    )
    return new_ent.T, new_est.reshape(-1), new_rel.T, new_rst.reshape(-1)


def solution(mesh):
    placed = (
        P(("groups", "rows"), "cols"),
        P(("groups", "rows")),
        P("groups", "cols"),
        P("groups"),
        P(("groups", "rows"), None, "edges", None, None),
        P(("groups", "rows"), "edges", None, "cols"),
        P(("groups", "rows"), "edges", None, "cols"),
        P(("groups", "rows"), "edges", None, "cols"),
        P(("groups", "rows"), "edges", None, None),
    )
    return jax.shard_map(
        local,
        mesh=mesh,
        in_specs=placed,
        out_specs=(
            P(("groups", "rows"), "cols"),
            P(("groups", "rows")),
            P("groups", "cols"),
            P("groups"),
        ),
        check_vma=False,
    )
```

profile of v0, /device:TPU:19, one launch (start us, length us, event | category | flops | bytes accessed | tf_op | source)
XLA Modules:
  0.0 99.0 jit_solution(15605584937251930610)
XLA Ops:
  0.6 1.3 %reshape.375.req = s32[1,512]{1,0:T(1,128)} reshape(s32[1,4,1,2,64]{4,3,2,1,0:T(2,128)} %param.13) | data formatting | bytes 4096 | tf_op jit(solution)/shard_map/reshape | solution.py:442
  2.0 0.1 broadcast_bitcast_fusion.1
  2.1 0.7 copy.13
  2.8 0.7 copy.15
  3.4 0.7 fusion.2
  4.1 1.3 %copy.16 = s32[1,1,2,512]{3,1,2,0:T(1,128)} copy(s32[1,1,2,512]{3,2,1,0:T(2,128)} %param.16) | data formatting | bytes 8192
  5.4 0.1 broadcast_bitcast_fusion
  5.5 0.7 copy.17
  6.2 0.7 fusion.neg
  6.9 86.5 %complex_step.1 = (f32[200,2048]{1,0:T(8,128)}, f32[1,2048]{1,0:T(1,128)}, f32[200,3072]{1,0:T(8,128)}, f32[1,3072]{1,0:T(1,128)}) custom-call(f32[200,2048]{1,0:T(8,128)} %bitcast.30, f32[1,2048]{1,0:T(1,128)} %bitcast.40, f32[200,3072]{1,0:T(8,128)} %bitcast.28, f32[1,3072]{1,0:T(1,128)} %bitcast.39, s32[1,512]{1,0:T(1,128)} %reshape.375.req, ...), custom_call_target="tpu_custom_call" | custom-call | tf_op jit(solution)/shard_map/complex_step/pallas_call | solution.py:425
  93.4 0.0 copy-start.2
  93.4 0.0 copy-start
  93.4 2.9 %copy.23 = f32[2048,200]{0,1:T(8,128)} copy(f32[2048,200]{0,1:T(8,128)} %bitcast.31) | data formatting | bytes 3276800
  96.3 0.0 copy-done.2
  96.4 0.6 copy.24
  97.0 0.0 copy-done
  97.0 0.0 copy-start.1
  97.0 1.4 %copy.25 = f32[3072,200]{0,1:T(8,128)} copy(f32[3072,200]{0,1:T(8,128)S(1)} %bitcast.29) | data formatting | bytes 4915200
  98.4 0.0 copy-done.1
  98.4 0.6 copy.26
  (3 shorter events, 0.0 us)
Async XLA Ops:
  93.4 2.9 %copy-start.2 = (f32[1,2048]{1,0:T(1,128)S(1)}, f32[1,2048]{1,0:T(1,128)}, u32[]{:S(2)}) copy-start(f32[1,2048]{1,0:T(1,128)} %get-tuple-element.9) | copy-start | bytes 24580
  93.4 3.5 %copy-start = (f32[200,3072]{1,0:T(8,128)S(1)}, f32[200,3072]{1,0:T(8,128)}, u32[]{:S(2)}) copy-start(f32[200,3072]{1,0:T(8,128)} %get-tuple-element.10) | copy-start | bytes 7372804
  97.0 1.4 %copy-start.1 = (f32[1,3072]{1,0:T(1,128)S(1)}, f32[1,3072]{1,0:T(1,128)}, u32[]{:S(2)}) copy-start(f32[1,3072]{1,0:T(1,128)} %get-tuple-element.11) | copy-start | bytes 36868
where the time goes:
time: 99.4 us; the launch traced here: 99 us
  Pallas kernels  86.5 us (87%)
  local copies, waits for them, and re-layouts  10.5 us (11%)
  other arithmetic  1.36 us (1%)
    pallas_call x1, Pallas kernels, local(): pl.pallas_call(functools.partial(kernel, n), out_shape=[jax.ShapeDtypeStr...  86.5 us
    unnamed x18, local copies, waits for them, and re-layouts  9.11 us

commit v1 on v0

--- a/solution.py
+++ b/solution.py
@@ -38,9 +38,12 @@
     return after, before
 
 
-def split_high(x):
-    high = x.astype(BF16)
-    return high, (x - high.astype(F32)).astype(BF16)
+def positions_of(slots, k, capacity, width):
+    if capacity & (capacity - 1):
+        owner = lax.div(slots, jnp.full_like(slots, capacity))
+    else:
+        owner = lax.shift_right_logical(slots, jnp.full_like(slots, capacity.bit_length() - 1))
+    return slots + owner * (width - capacity) + k * capacity
 
 
 def pad_rows(x, rows):
@@ -56,7 +59,7 @@
 def kernel(
     n, ent, est, rel, rst, req, head, tail, rid, neg,
     new_ent, new_est, new_rel, new_rst,
-    relb, entb, fetg, fet, allreq, oh_head, oh_tail, oh_rel, share, rho, rho_hi, rho_lo,
+    relb, entb, fetg, fet, allreq, oh_head, oh_tail, oh_rel, share, rho, rho_grads,
     slot_grad, ent_send, ent_in, grad_out, grad_in, sq_ent, sq_ent_in,
     pair_out, pair_in, pair_sum, x_out, x_in, z_out, z_in, total, sq_rel, sq_rel_in,
     s_relb, r_relb, s_req, r_req, s_fet, r_fet, s_ent, r_ent, s_grad, r_grad,
@@ -93,9 +96,9 @@
 
     entb[...] = pad_rows(ent[...], HP).astype(BF16)
     relb[c] = pad_rows(rel[...], HP).astype(BF16)
-    allreq[e] = req[...]
     for w in range(R):
-        ids = req[:, w * PW : (w + 1) * PW]
+        ids = jnp.concatenate([req[w, k : k + 1, :] for k in range(K)], axis=1)
+        allreq[e, :, w * PW : (w + 1) * PW] = ids
         fetg[w] = dot(entb[...], one_hot(0, ent.shape[1], ids)).astype(BF16)
     pl.semaphore_wait(barrier, R * E * 2 - 1)
 
@@ -122,24 +125,30 @@
     sent += fetch + [relation_copy] + request_copies
 
     positions = R * PW
-    negatives = neg.shape[1] // K
+    negatives = neg.shape[1]
     for k in range(K):
         slots = lax.broadcasted_iota(jnp.int32, (positions, 128), 0)
         hits = jnp.zeros((positions, 128), F32)
-        for at in range(k * negatives, (k + 1) * negatives, 128):
-            hits += jnp.where(slots == neg[:, at : at + 128], 1.0, 0.0)
+        for at in range(0, negatives, 128):
+            ids = positions_of(neg[k : k + 1, at : at + 128], k, n.capacity, PW)
+            hits += jnp.where(slots == ids, 1.0, 0.0)
         share[k] = jnp.sum(hits, axis=1, keepdims=True) / negatives
 
-    edges = head.shape[1]
+    per_block = head.shape[1]
+    edges = K * per_block
     step = n.step
-
-    @pl.loop(0, edges // step)
-    def _(t):
-        cols = pl.ds(pl.multiple_of(t * step, step), step)
-        oh_head[:, cols] = one_hot(0, positions, head[:, cols])
-        oh_tail[:, cols] = one_hot(0, positions, tail[:, cols])
-        oh_rel[:, cols] = one_hot(0, rel.shape[1], rid[:, cols])
-        rho[c, :, cols] = dot(relb[c], oh_rel[:, cols]).astype(BF16)
+    for k in range(K):
+
+        @pl.loop(0, per_block // step)
+        def _(t):
+            ids = pl.ds(pl.multiple_of(t * step, step), step)
+            cols = pl.ds(pl.multiple_of(k * per_block + t * step, step), step)
+            heads = positions_of(head[k : k + 1, ids], k, n.capacity, PW)
+            tails = positions_of(tail[k : k + 1, ids], k, n.capacity, PW)
+            oh_head[:, cols] = one_hot(0, positions, heads)
+            oh_tail[:, cols] = one_hot(0, positions, tails)
+            oh_rel[:, cols] = one_hot(0, rel.shape[1], rid[k : k + 1, ids])
+            rho[c, :, cols] = dot(relb[c], oh_rel[:, cols]).astype(BF16)
 
     relation_copy.wait_recv()
 
@@ -152,7 +161,6 @@
         copy.wait_recv()
 
     slot_grad[...] = jnp.zeros_like(slot_grad)
-    per_block = edges // K
     for k in range(K):
 
         @pl.loop(0, per_block // step)
@@ -180,14 +188,10 @@
             h_re = jnp.where(even, h, h_before)
             h_im = jnp.where(even, -h_after, h)
             rho_grad = g * h_re - g_swap * h_im
-            high, low = split_high(rho_grad)
-            rho_hi[:, :, cols] = high.reshape(2, HP, step)
-            rho_lo[:, :, cols] = low.reshape(2, HP, step)
+            rho_grads[:, :, cols] = rho_grad.astype(BF16).reshape(2, HP, step)
             acc = dot_nt(query_b, weight)
-            high, low = split_high(head_grad)
-            acc += dot_nt(high, oh_head[:, cols]) + dot_nt(low, oh_head[:, cols])
-            high, low = split_high(pos_weight * query)
-            acc += dot_nt(high, oh_tail[:, cols]) + dot_nt(low, oh_tail[:, cols])
+            acc += dot_nt(head_grad.astype(BF16), oh_head[:, cols])
+            acc += dot_nt((pos_weight * query).astype(BF16), oh_tail[:, cols])
             slot_grad[...] += acc.reshape(2, HP, positions)
 
     ent_send[...] = slot_grad[pc]
@@ -203,7 +207,7 @@
 
     def dense(which, de, p):
         hot = oh_rel[pl.ds(place(de, p), L), :]
-        return dot_nt(rho_hi[which], hot) + dot_nt(rho_lo[which], hot)
+        return dot_nt(rho_grads[which], hot)
 
     def send_pair(de, p):
         i = de * PIECES + p
@@ -385,7 +389,7 @@
     n = Sizes()
     n.rows, n.edges = lax.axis_size("rows"), lax.axis_size("edges")
     n.blocks = requests.shape[3]
-    capacity = requests.shape[4]
+    capacity = n.capacity = requests.shape[4]
     shard_rows, half = entities.shape
     types = relations.shape[0]
     n.width = n.blocks * capacity
@@ -397,11 +401,6 @@
     positions = n.rows * n.width
     edges = n.blocks * head_slot.shape[3]
 
-    def spots(slots):
-        slots = slots[0, 0]
-        block = jnp.arange(n.blocks, dtype=jnp.int32)[:, None]
-        return ((slots // capacity) * n.width + block * capacity + slots % capacity).reshape(1, -1)
-
     HP, R, E, PC, L = n.padded, n.rows, n.edges, n.pieces, n.lanes
     V = pltpu.VMEM
     sem = lambda k: pltpu.SemaphoreType.DMA((max(k, 1),))
@@ -410,7 +409,7 @@
         V((2, HP, positions), BF16), V((E, 1, positions), jnp.int32),
         V((positions, edges), BF16), V((positions, edges), BF16), V((types, edges), BF16),
         V((n.blocks, positions, 1), F32), V((2, HP, edges), BF16),
-        V((2, HP, edges), BF16), V((2, HP, edges), BF16),
+        V((2, HP, edges), BF16),
         V((2, HP, positions), F32), V((HP, positions), F32), V((HP, positions), F32),
         V((R, HP, n.width), BF16), V((E, HP, positions), BF16),
         V((1, shard_rows), F32), V((1, shard_rows), F32),
@@ -439,8 +438,7 @@
         name="complex_step",
     )(
         entities.T, entity_state.reshape(1, -1), relations.T, relation_state.reshape(1, -1),
-        requests.reshape(1, -1), spots(head_slot), spots(tail_slot),
-        relation_ids.reshape(1, -1), spots(negative_slot),
+        requests[0, :, 0], head_slot[0, 0], tail_slot[0, 0], relation_ids[0, 0], negative_slot[0, 0],
     )
     return new_ent.T, new_est.reshape(-1), new_rel.T, new_rst.reshape(-1)
 

time: 99.4 us -> 93.3 us (0.939)
  the two profiles are of different devices: /device:TPU:19 before, /device:TPU:1 now
where the time goes in v1:
time: 93.3 us; the launch traced here: 93.1 us
  Pallas kernels  86.9 us (93%)
  local copies, waits for them, and re-layouts  5.56 us (6%)
    pallas_call x1, Pallas kernels, local(): pl.pallas_call(functools.partial(kernel, n), out_shape=[jax.ShapeDtypeStr...  86.9 us
    unnamed x10, local copies, waits for them, and re-layouts  5.56 us

profile of v1, /device:TPU:1, one launch (start us, length us, event | category | flops | bytes accessed | tf_op | source)
XLA Modules:
  0.0 93.1 jit_solution(14442037125928438164)
XLA Ops:
  0.6 86.9 %complex_step.1 = (f32[200,2048]{1,0:T(8,128)}, f32[1,2048]{1,0:T(1,128)}, f32[200,3072]{1,0:T(8,128)}, f32[1,3072]{1,0:T(1,128)}) custom-call(f32[200,2048]{1,0:T(8,128)} %bitcast.16, f32[1,2048]{1,0:T(1,128)} %bitcast.20, f32[200,3072]{1,0:T(8,128)} %bitcast.13, f32[1,3072]{1,0:T(1,128)} %bitcast.18, s32[4,2,64]{2,1,0:T(2,128)} %bitcast.22, ...), custom_call_target="tpu_custom_call" | custom-call | tf_op jit(solution)/shard_map/complex_step/pallas_call | solution.py:424
  87.5 0.0 copy-start.2
  87.5 0.0 copy-start
  87.6 2.9 %copy.17 = f32[2048,200]{0,1:T(8,128)} copy(f32[2048,200]{0,1:T(8,128)} %bitcast.15) | data formatting | bytes 3276800
  90.5 0.0 copy-done.2
  90.5 0.6 copy.18
  91.1 0.0 copy-done
  91.1 0.0 copy-start.1
  91.1 1.4 %copy.19 = f32[3072,200]{0,1:T(8,128)} copy(f32[3072,200]{0,1:T(8,128)S(1)} %bitcast.14) | data formatting | bytes 4915200
  92.5 0.0 copy-done.1
  92.5 0.6 copy.20
Async XLA Ops:
  87.5 2.9 %copy-start.2 = (f32[1,2048]{1,0:T(1,128)S(1)}, f32[1,2048]{1,0:T(1,128)}, u32[]{:S(2)}) copy-start(f32[1,2048]{1,0:T(1,128)} %get-tuple-element.9) | copy-start | bytes 24580
  87.5 3.5 %copy-start = (f32[200,3072]{1,0:T(8,128)S(1)}, f32[200,3072]{1,0:T(8,128)}, u32[]{:S(2)}) copy-start(f32[200,3072]{1,0:T(8,128)} %get-tuple-element.10) | copy-start | bytes 7372804
  91.1 1.4 %copy-start.1 = (f32[1,3072]{1,0:T(1,128)S(1)}, f32[1,3072]{1,0:T(1,128)}, u32[]{:S(2)}) copy-start(f32[1,3072]{1,0:T(1,128)} %get-tuple-element.11) | copy-start | bytes 36868

commit v2 on v1

--- a/solution.py
+++ b/solution.py
@@ -200,7 +200,8 @@
     sent.append(entity_pair)
 
     def place(de, p):
-        return pl.multiple_of((lax.rem(e + de, E) * PIECES + p) * L, L)
+        piece = lax.rem(r + 1 + p, R) if full else p
+        return pl.multiple_of((lax.rem(e + de, E) * PIECES + piece) * L, L)
 
     order = [(de, p) for de in list(range(1, E)) + [0] for p in range(PIECES)]
     pairs = {}
@@ -257,7 +258,6 @@
             sent.append(copy)
         else:
             pair_sum[p] = own
-    grads = entity_out()
 
     def over_edges(p):
         acc = pair_sum[p]
@@ -276,8 +276,10 @@
 
         @when(full, p < PIECES)
         def _():
-            z_out[dr - 1] = over_edges(p).astype(BF16)
+            z_out[dr - 1] = over_edges(dr - 1 if full else p).astype(BF16)
             z_copy(dr).start()
+
+    grads = entity_out()
 
     def mine(dr):
         return e * PIECES + lax.rem(r + R - dr, R)
@@ -297,7 +299,7 @@
 
     @when(full, r < PIECES)
     def _():
-        acc = over_edges(r)
+        acc = over_edges(R - 1 if full else r)
         for dr in range(1, R):
             z_copy(dr).wait_recv()
             acc += z_in[dr - 1].astype(F32)

time: 93.3 us -> 89.8 us (0.962)
  the two profiles are of different devices: /device:TPU:1 before, /device:TPU:19 now
where the time goes in v2:
time: 89.8 us; the launch traced here: 89.2 us
  Pallas kernels  83 us (92%)
  local copies, waits for them, and re-layouts  5.56 us (6%)
    pallas_call x1, Pallas kernels, local(): pl.pallas_call(functools.partial(kernel, n), out_shape=[jax.ShapeDtypeStr...  83 us
    unnamed x10, local copies, waits for them, and re-layouts  5.56 us

profile of v2, /device:TPU:19, one launch (start us, length us, event | category | flops | bytes accessed | tf_op | source)
XLA Modules:
  0.0 89.2 jit_solution(5777313029682221225)
XLA Ops:
  0.6 83.0 %complex_step.1 = (f32[200,2048]{1,0:T(8,128)}, f32[1,2048]{1,0:T(1,128)}, f32[200,3072]{1,0:T(8,128)}, f32[1,3072]{1,0:T(1,128)}) custom-call(f32[200,2048]{1,0:T(8,128)} %bitcast.16, f32[1,2048]{1,0:T(1,128)} %bitcast.20, f32[200,3072]{1,0:T(8,128)} %bitcast.13, f32[1,3072]{1,0:T(1,128)} %bitcast.18, s32[4,2,64]{2,1,0:T(2,128)} %bitcast.22, ...), custom_call_target="tpu_custom_call" | custom-call | tf_op jit(solution)/shard_map/complex_step/pallas_call | solution.py:426
  83.7 0.0 copy-start.2
  83.7 0.0 copy-start
  83.7 2.9 %copy.17 = f32[2048,200]{0,1:T(8,128)} copy(f32[2048,200]{0,1:T(8,128)} %bitcast.15) | data formatting | bytes 3276800
  86.6 0.0 copy-done.2
  86.6 0.6 copy.18
  87.2 0.0 copy-done
  87.2 0.0 copy-start.1
  87.2 1.4 %copy.19 = f32[3072,200]{0,1:T(8,128)} copy(f32[3072,200]{0,1:T(8,128)S(1)} %bitcast.14) | data formatting | bytes 4915200
  88.6 0.0 copy-done.1
  88.6 0.6 copy.20
Async XLA Ops:
  83.7 2.9 %copy-start.2 = (f32[1,2048]{1,0:T(1,128)S(1)}, f32[1,2048]{1,0:T(1,128)}, u32[]{:S(2)}) copy-start(f32[1,2048]{1,0:T(1,128)} %get-tuple-element.9) | copy-start | bytes 24580
  83.7 3.5 %copy-start = (f32[200,3072]{1,0:T(8,128)S(1)}, f32[200,3072]{1,0:T(8,128)}, u32[]{:S(2)}) copy-start(f32[200,3072]{1,0:T(8,128)} %get-tuple-element.10) | copy-start | bytes 7372804
  87.2 1.4 %copy-start.1 = (f32[1,3072]{1,0:T(1,128)S(1)}, f32[1,3072]{1,0:T(1,128)}, u32[]{:S(2)}) copy-start(f32[1,3072]{1,0:T(1,128)} %get-tuple-element.11) | copy-start | bytes 36868
